TPU v7x, 256 devices: a whole 4x4x8 slice. The times are simulated.
256 devices in a mesh: src: 8 (over z_lo, y), tgt: 32 (over x, z_hi, core).
Axes of the slice: x: 4, y: 4, z: 8 (z_hi: 4, z_lo: 2; z = z_hi * 2 + z_lo), core: 2. Of those that a mesh axis runs over, the one named last changes fastest.
Arguments:
- source_feat: float32 [2048, 256], P(('src', 'tgt')), may hold values from -6 to 6
- target_feat: float32 [131072, 256], P('tgt'), may hold values from -6 to 6
- target_order: int32 [131072], P('tgt'), may hold values from 0 to 131071, as said below
- window_id: int32 [2048], replicated, may hold values from 0 to 80, as said below
- latent_query: float32 [8, 128], replicated, may hold values from -120 to 120
- patch_weight: float32 [64, 128], replicated, may hold values from -0.75 to 0.75
- patch_embed_bias: float32 [128], replicated, may hold values from -4 to 4
- key_weight: float32 [128, 128], replicated, may hold values from -0.5 to 0.5
- value_matrix: float32 [128, 128], replicated, may hold values from -0.5 to 0.5
- window_query: float32 [128, 128], replicated, may hold values from -4 to 4
- window_key: float32 [128, 128], replicated, may hold values from -0.5 to 0.5
- window_value: float32 [128, 128], replicated, may hold values from -0.5 to 0.5
- window_out: float32 [128, 128], replicated, may hold values from -0.5 to 0.5
- norm_gain: float32 [128], replicated, may hold values from 0.25 to 1.75
- up_weight: float32 [128, 512], replicated, may hold values from -0.5 to 0.5
- up_bias: float32 [512], replicated, may hold values from -4 to 4
- down_weight: float32 [512, 128], replicated, may hold values from -0.25 to 0.25
Outputs:
- cost_memory: float32 [2048, 8, 128], P(('src', 'tgt'))
Inputs may be any that keep to these rules, and one draw needn't show every extreme that they name: `target_order`: each aligned block of 4096 entries holds every index of that block exactly once. `window_id`: source pixels are numbered row after row, 64 to a row; pixels with equal ids lie within one band of 256 consecutive pixels or within two neighbouring bands.
All inputs are finite; a program needn't handle non-finite values.
Results may differ from a plain program's by a relative error of at most 0.0003.
Values sent between devices are 32-bit elements; how exact they have to be, the bound alone decides.
A program may use at most 192 MiB of HBM per device.

v0:
```python
import math

import jax
import jax.numpy as jnp
from jax import lax
from jax.sharding import PartitionSpec as P

HIGH_PRECISION = lax.Precision.HIGHEST


def merged(value, axis, join):
    pieces = jax.tree.map(lambda part: lax.all_gather(part, axis), value)
    head = jax.tree.map(lambda part: part[0], pieces)
    tail = jax.tree.map(lambda part: part[1:], pieces)
    total, _ = lax.scan(lambda total, slab: (join(total, slab), None), head, tail)
    return total


def passed_along(block, axis, distance):
    devices = range(lax.axis_size(axis))
    route = [(i - distance, i) for i in devices if i - distance in devices]
    return lax.ppermute(block, axis, route)


def combine_softmax(first, second):
    peak_one, total_one, summed_one = first
    peak_two, total_second, summed_two = second
    peak = jnp.maximum(peak_one, peak_two)
    factor_one = jnp.exp(peak_one - peak)
    factor_two = jnp.exp(peak_two - peak)
    row_count = summed_one.shape[0]
    latents = peak_one.shape[1]
    part_one = summed_one.reshape(row_count, latents, -1) * factor_one[:, :, None]
    part_two = summed_two.reshape(row_count, latents, -1) * factor_two[:, :, None]
    total = total_one * factor_one + total_second * factor_two
    return (peak, total, (part_one + part_two).reshape(row_count, -1))


def local(
    source_feat,
    target_feat,
    target_order,
    window_id,
    latent_query,
    patch_weight,
    patch_embed_bias,
    key_weight,
    value_matrix,
    window_query,
    window_key,
    window_value,
    window_out,
    norm_gain,
    up_weight,
    up_bias,
    down_weight,
):
    tgt_rank = lax.axis_index("tgt")
    src_rank = lax.axis_index("src")
    tgt_count = lax.axis_size("tgt")
    local_count = target_feat.shape[0]
    patch_len, width = patch_weight.shape
    latents = latent_query.shape[0]
    local_order = target_order - tgt_rank * local_count
    ordered = jnp.take(target_feat, local_order, axis=0)
    band = lax.all_gather(source_feat, "tgt", axis=0, tiled=True)
    band_len, channels = band.shape
    share = band_len // tgt_count
    key_query = jnp.dot(key_weight, latent_query.T, precision=HIGH_PRECISION) / math.sqrt(width)

    def partial_block(rows):
        cost = jnp.dot(rows, ordered.T, precision=HIGH_PRECISION) / math.sqrt(channels)
        patches = cost.reshape(rows.shape[0], -1, patch_len)
        source = (
            jnp.einsum("bpq,qd->bpd", patches, patch_weight, precision=HIGH_PRECISION)
            + patch_embed_bias
        )
        scores = jnp.einsum("bpd,dk->bkp", source, key_query, precision=HIGH_PRECISION)
        peak = jnp.max(scores, axis=-1)
        weights = jnp.exp(scores - peak[:, :, None])
        total = jnp.sum(weights, axis=-1)
        summed_rows = jnp.einsum("bkp,bpx->bkx", weights, source, precision=HIGH_PRECISION)
        return (peak, total, summed_rows.reshape(rows.shape[0], -1))

    block_rows = math.gcd(band_len, 256)
    peak, total, summed_rows = lax.map(partial_block, band.reshape(-1, block_rows, channels))
    peak = peak.reshape(band_len, latents)
    total = total.reshape(band_len, latents)
    summed_rows = summed_rows.reshape(band_len, -1)
    peak, total, summed_rows = merged((peak, total, summed_rows), "tgt", combine_softmax)
    mean = summed_rows.reshape(band_len, latents, -1) / total[:, :, None]
    latent = jnp.einsum("skd,de->ske", mean, value_matrix, precision=HIGH_PRECISION)
    mine = lax.dynamic_slice_in_dim(latent, tgt_rank * share, share, 0)
    before = passed_along(latent, "src", 1)
    after = passed_along(latent, "src", -1)
    neighbourhood = jnp.concatenate([before, latent, after], axis=0)
    query = jnp.einsum("skd,de->kse", mine, window_query, precision=HIGH_PRECISION)
    keys = jnp.einsum("skd,de->kse", neighbourhood, window_key, precision=HIGH_PRECISION)
    values = jnp.einsum("skd,de->kse", neighbourhood, window_value, precision=HIGH_PRECISION)
    outside = jnp.full((band_len,), -1, jnp.int32)
    padded_ids = jnp.concatenate([outside, window_id, outside], axis=0)
    key_ids = lax.dynamic_slice_in_dim(padded_ids, src_rank * band_len, 3 * band_len, 0)
    query_ids = lax.dynamic_slice_in_dim(
        window_id, src_rank * band_len + tgt_rank * share, share, 0
    )
    scores = jnp.einsum("kse,kte->kst", query, keys, precision=HIGH_PRECISION) / math.sqrt(width)
    scores = jnp.where((query_ids[:, None] == key_ids[None, :])[None, :, :], scores, -jnp.inf)
    weights = jax.nn.softmax(scores, axis=-1)
    mixed = jnp.einsum("kst,kte->kse", weights, values, precision=HIGH_PRECISION)
    resid = mine + jnp.einsum("kse,ed->skd", mixed, window_out, precision=HIGH_PRECISION)
    center = jnp.mean(resid, axis=-1, keepdims=True)
    spread_values = jnp.mean((resid - center) ** 2, axis=-1, keepdims=True)
    normed = (resid - center) / jnp.sqrt(spread_values + 1e-05) * norm_gain
    hidden = jax.nn.gelu(
        jnp.einsum("skd,df->skf", normed, up_weight, precision=HIGH_PRECISION) + up_bias
    )
    return resid + jnp.einsum("skf,fd->skd", hidden, down_weight, precision=HIGH_PRECISION)


def solution(mesh):
    placed = (
        P(("src", "tgt"), None),
        P("tgt", None),
        P("tgt"),
        P(),
        P(),
        P(),
        P(),
        P(),
        P(),
        P(),
        P(),
        P(),
        P(),
        P(),
        P(),
        P(),
        P(),
    )
    return jax.shard_map(
        local, mesh=mesh, in_specs=placed, out_specs=P(("src", "tgt"), None, None), check_vma=False
    )
```

profile of v0, /device:TPU:1, one launch (start us, length us, event | category | flops | bytes accessed | tf_op | source)
XLA Modules:
  0.0 495.9 jit_solution(1512736816732608231)
XLA Ops:
  8.0 49.6 %all_gather.12 = f32[256,256]{1,0:T(8,128)S(1)} all-gather(f32[8,256]{1,0:T(8,128)} %param.19), channel_id=1, replica_groups=mesh['src'=8,'tgt'=32] {'tgt'}, dimensions={0}, use_global_device_ids=true | all-gather | bytes 270336 | tf_op jit(solution)/shard_map/all_gather | solution.py:66
  57.6 18.4 %gather_fusion = f32[4096,256]{1,0:T(8,128)} fusion(f32[4096,256]{1,0:T(8,128)} %param.20, s32[4096]{0:T(1024)S(1)} %fusion.53), kind=kCustom, calls=%fused_computation | custom fusion | bytes 8404992 | tf_op jit(solution)/shard_map/jit(_take)/gather | solution.py:65
  76.2 6.6 %convolution_multiply_fusion = f32[4096,256]{1,0:T(8,128)S(1)} fusion(f32[256,256]{1,0:T(8,128)S(1)} %all_gather.12, f32[4096,256]{1,0:T(8,128)} %gather_fusion, pred[4096]{0:T(1024)(128)(4,1)S(1)} %compare_and_fusion), kind=kOutput, calls=%fused_computation.12 | convolution fusion | flops 3223322624 | bytes 8654848 | tf_op jit(solution)/shard_map/while/body/eval_jaxpr/dot_general | solution.py:72
  82.8 13.7 %broadcast_add_fusion = f32[256,64,128]{2,0,1:T(8,128)S(1)} fusion(f32[128]{0:T(128)S(1)} %copy-done.12, f32[256,64,64]{0,2,1:T(8,128)S(1)} %bitcast.110, f32[64,128]{1,0:T(8,128)S(1)} %copy-done.8), kind=kOutput, calls=%fused_computation.13 | convolution fusion | flops 1612709888 | bytes 12616192 | tf_op jit(solution)/shard_map/while/body/eval_jaxpr/bpq,qd->bpd/dot_general | solution.py:75
  96.5 6.9 %fusion.60 = (f32[256,8]{0,1:T(8,128)S(1)}, f32[256,8,64]{0,1,2:T(8,128)S(1)}) fusion(f32[128,8,1]{0,1,2:T(8,128)S(1)} %fusion.24, f32[256,64,128]{2,0,1:T(8,128)S(1)} %broadcast_add_fusion), kind=kOutput, calls=%fused_computation.82 | convolution fusion | flops 201455616 | bytes 8925184 | tf_op jit(solution)/shard_map/while/body/eval_jaxpr/bpd,dk->bkp/dot_general | solution.py:78
  104.0 14.8 %fusion.3 = f32[256,8,128]{2,1,0:T(8,128)S(1)} fusion(f32[256,8,64]{2,1,0:T(8,128)S(1)} %copy.28, f32[256,64,128]{2,0,1:T(8,128)} %copy-done.1), kind=kOutput, calls=%fused_computation.10 | convolution fusion | flops 201326592 | bytes 9961472 | tf_op jit(solution)/shard_map/while/body/eval_jaxpr/bkp,bpx->bkx/dot_general | solution.py:82
  119.9 42.2 %all-gather.1 = f32[8192,8]{0,1:T(8,128)S(1)} all-gather(f32[256,8]{0,1:T(8,128)S(1)} %get-tuple-element.90), channel_id=3, replica_groups=mesh['src'=8,'tgt'=32] {'tgt'}, dimensions={0}, use_global_device_ids=true | all-gather | bytes 270336 | tf_op jit(solution)/shard_map/all_gather | solution.py:12
  162.2 43.0 %all-gather = f32[8192,8]{0,1:T(8,128)S(1)} all-gather(f32[256,8]{0,1:T(8,128)S(1)} %get-tuple-element.92), channel_id=2, replica_groups=mesh['src'=8,'tgt'=32] {'tgt'}, dimensions={0}, use_global_device_ids=true | all-gather | bytes 270336 | tf_op jit(solution)/shard_map/all_gather | solution.py:12
  205.2 116.1 %all-gather.4.cloned.1.call-done = f32[32,256,1024]{2,1,0:T(8,128)} async-done(((f32[1,256,1024]{2,1,0:T(8,128)}), f32[32,256,1024]{2,1,0:T(8,128)}) %all-gather.4.cloned.1.call-update) | async-done | bytes 33554448 | tf_op jit(solution)/shard_map/all_gather | solution.py:12
  321.2 23.0 %slice.35 = f32[31,256,1024]{2,1,0:T(8,128)} slice(f32[32,256,1024]{2,1,0:T(8,128)} %all-gather.4.cloned.1.call-done), slice={[1:32], [0:256], [0:1024]} | slice | bytes 65011712 | tf_op jit(solution)/shard_map/slice | solution.py:14
  345.6 97.2 %while.2 = (s32[]{:T(128)}, f32[256,8]{0,1:T(8,128)S(1)}, f32[256,8]{0,1:T(8,128)S(1)}, f32[256,1024]{1,0:T(8,128)S(1)}, f32[31,256,8]{1,2,0:T(8,128)S(1)}, /*in...) while((s32[]{:T(128)}, f32[256,8]{0,1:T(8,128)S(1)}, f32[256,8]{0,1:T(8,128)S(1)}, ...), condition=%wide.region_3.4_spmd, body=%wide.region_2.3_spmd.sunk | while | flops 798722 | bytes 7454813 | solution.py:15
  346.5 2.2 fusion.77
  349.7 2.2 fusion.77
  352.8 2.2 fusion.77
  355.9 2.2 fusion.77
  368.5 2.2 fusion.77
  371.6 2.2 fusion.77
  374.8 2.2 fusion.77
  387.3 2.2 fusion.77
  390.4 2.2 fusion.77
  393.6 2.2 fusion.77
  409.2 2.2 fusion.77
  412.4 2.2 fusion.77
  428.1 2.2 fusion.77
  431.2 2.2 fusion.77
  434.3 2.2 fusion.77
  443.8 4.8 collective-permute-start
  450.6 20.3 %collective-permute-done = f32[256,8,128]{2,0,1:T(8,128)S(1)} collective-permute-done((f32[256,8,128]{2,0,1:T(8,128)S(1)}, f32[256,8,128]{2,0,1:T(8,128)S(1)}, u32[]{:S(2)}, u32[]{:S(2)}) %collective-permute-start) | collective-permute-done | bytes 1048608 | tf_op jit(solution)/shard_map/ppermute | solution.py:22
  470.9 3.9 collective-permute-done.1
  474.7 2.7 fusion.46
  477.5 2.8 fusion.61
  480.7 4.2 fusion.14
  (233 shorter events, 75.6 us)
Async XLA Ops:
  6.5 481.0 %copy-start = (f32[128,512]{1,0:T(8,128)S(1)}, f32[128,512]{1,0:T(8,128)}, u32[]{:S(2)}) copy-start(f32[128,512]{1,0:T(8,128)} %param.33) | copy-start | bytes 786436
  6.5 314.7 %all-gather.4.cloned.1.call-start = ((), (), s32[]{:S(2)}) async-start(), calls=%async_computation | async-start | bytes 34603008 | tf_op jit(solution)/shard_map/all_gather | solution.py:12
  57.6 18.4 %copy-start.5 = (f32[128,128]{1,0:T(8,128)S(1)}, f32[128,128]{1,0:T(8,128)}, u32[]{:S(2)}) copy-start(f32[128,128]{1,0:T(8,128)} %param.26) | copy-start | bytes 196612
  57.6 18.4 %copy-start.10 = (f32[8,128]{1,0:T(8,128)S(1)}, f32[8,128]{1,0:T(8,128)}, u32[]{:S(2)}) copy-start(f32[8,128]{1,0:T(8,128)} %param.23) | copy-start | bytes 12292
  76.2 6.6 %copy-start.8 = (f32[64,128]{1,0:T(8,128)S(1)}, f32[64,128]{1,0:T(8,128)}, u32[]{:S(2)}) copy-start(f32[64,128]{1,0:T(8,128)} %param.24) | copy-start | bytes 98308
  76.2 6.6 %copy-start.12 = (f32[128]{0:T(128)S(1)}, f32[128]{0:T(128)}, u32[]{:S(2)}) copy-start(f32[128]{0:T(128)} %param.25) | copy-start | bytes 1540
  96.5 6.9 %copy-start.1 = (f32[256,64,128]{2,0,1:T(8,128)}, f32[256,64,128]{2,0,1:T(8,128)S(1)}, u32[]{:S(2)}) copy-start(f32[256,64,128]{2,0,1:T(8,128)S(1)} %broadcast_add_fusion) | copy-start | bytes 25165828
  345.5 97.3 %copy-start.14 = (f32[128,128]{1,0:T(8,128)S(1)}, f32[128,128]{1,0:T(8,128)}, u32[]{:S(2)}) copy-start(f32[128,128]{1,0:T(8,128)} %param.27) | copy-start | bytes 196612
  345.5 104.6 %copy-start.9 = (s32[2048]{0:T(1024)S(1)}, s32[2048]{0:T(1024)}, u32[]{:S(2)}) copy-start(s32[2048]{0:T(1024)} %param.22) | copy-start | bytes 24580
  345.5 104.9 %copy-start.6 = (f32[128,128]{1,0:T(8,128)S(1)}, f32[128,128]{1,0:T(8,128)}, u32[]{:S(2)}) copy-start(f32[128,128]{1,0:T(8,128)} %param.28) | copy-start | bytes 196612
  345.5 129.2 %copy-start.3 = (f32[128,128]{1,0:T(8,128)S(1)}, f32[128,128]{1,0:T(8,128)}, u32[]{:S(2)}) copy-start(f32[128,128]{1,0:T(8,128)} %param.29) | copy-start | bytes 196612
  443.8 27.1 %collective-permute-start = (f32[256,8,128]{2,0,1:T(8,128)S(1)}, f32[256,8,128]{2,0,1:T(8,128)S(1)}, u32[]{:S(2)}, u32[]{:S(2)}) collective-permute-start(f32[256,8,128]{2,0,1:T(8,128)S(1)} %fusion.25), channel_id=1, source_target_pairs={{0,32},{32,64},{64,96},{96,128},{128,160},{160,192},{192,224},{1,3... | collective-permute-start | bytes 3145736 | tf_op jit(solution)/shard_map/ppermute | solution.py:22
  448.6 26.1 %collective-permute-start.1 = (f32[256,8,128]{2,0,1:T(8,128)S(1)}, f32[256,8,128]{2,0,1:T(8,128)S(1)}, u32[]{:S(2)}, u32[]{:S(2)}) collective-permute-start(f32[256,8,128]{2,0,1:T(8,128)S(1)} %fusion.25), channel_id=1, source_target_pairs={{32,0},{64,32},{96,64},{128,96},{160,128},{192,160},{224,192},{33,... | collective-permute-start | bytes 3145736 | tf_op jit(solution)/shard_map/ppermute | solution.py:22
  477.4 3.2 copy-start.4
  480.6 6.3 %copy-start.7 = (f32[128,128]{1,0:T(8,128)S(1)}, f32[128,128]{1,0:T(8,128)}, u32[]{:S(2)}) copy-start(f32[128,128]{1,0:T(8,128)} %param.31) | copy-start | bytes 196612
  480.7 6.8 %copy-start.13 = (f32[128]{0:T(128)S(1)}, f32[128]{0:T(128)}, u32[]{:S(2)}) copy-start(f32[128]{0:T(128)} %param.32) | copy-start | bytes 1540
  480.7 6.9 %copy-start.11 = (f32[512]{0:T(512)S(1)}, f32[512]{0:T(512)}, u32[]{:S(2)}) copy-start(f32[512]{0:T(512)} %param.34) | copy-start | bytes 6148
  480.7 7.2 %copy-start.2 = (f32[512,128]{1,0:T(8,128)S(1)}, f32[512,128]{1,0:T(8,128)}, u32[]{:S(2)}) copy-start(f32[512,128]{1,0:T(8,128)} %param.35) | copy-start | bytes 786436
Sparse Core Ops, SparseCore 0:
  120.1 201.1 all-gather.3
where the time goes:
time: 501 us; the launch traced here: 496 us
  waiting for transfers between devices  140 us (28%)
  blocking collectives  135 us (27%)
  local copies, waits for them, and re-layouts  73.6 us (15%)
  other arithmetic  69.9 us (14%)
  matrix products  55.9 us (11%)
  between operations  14 us (3%)
  starting transfers between devices  6.33 us (1%)
    all_gather x1, waiting for transfers between devices, merged(): pieces = jax.tree.map(lambda part: lax.all_gather(part, axis), value)  116 us
    all_gather x2, blocking collectives, merged(): pieces = jax.tree.map(lambda part: lax.all_gather(part, axis), value)  85.2 us
    add x31, other arithmetic, combine_softmax(): return (peak, total, (part_one + part_two).reshape(row_count, -1))  66.9 us
    all_gather x1, blocking collectives, local(): band = lax.all_gather(source_feat, 'tgt', axis=0, tiled=True)  49.6 us
    ppermute x2, waiting for transfers between devices, passed_along(): return lax.ppermute(block, axis, route)  24.1 us
    slice x3, local copies, waits for them, and re-layouts, merged(): tail = jax.tree.map(lambda part: part[1:], pieces)  23 us
    gather x1, local copies, waits for them, and re-layouts, local(): ordered = jnp.take(target_feat, local_order, axis=0)  18.4 us
    dot_general x1, matrix products, partial_block(): jnp.einsum('bkp,bpx->bkx', weights, source, precision=HIGH_PRECISION)  14.8 us
  transfers between devices with their start and end apart: 3, of which 3 were waited for; matrix products, arithmetic and copies ran while one was open for 0% of the time, Pallas kernels for 0%

commit v1 on v0

v1 whole, which is shorter than its diff:
```python
import functools
import math

import jax
import jax.numpy as jnp
from jax import lax
from jax.experimental import pallas as pl
from jax.experimental.pallas import tpu as pltpu
from jax.sharding import PartitionSpec as P

HI = lax.Precision.HIGHEST
MESH = pl.DeviceIdType.MESH
F32 = jnp.float32

NX, NH, NC = 4, 4, 2
BAND = 256
C = 256
D = 128
K = 8
PATCH = 64
TARGETS = 4096
PATCHES = TARGETS // PATCH
ROWS = 8
QC = PATCH // NH
PIX = BAND // NH


def nn(a, b):
    return lax.dot_general(a, b, (((1,), (0,)), ((), ())), precision=HI, preferred_element_type=F32)


def nt(a, b):
    return lax.dot_general(a, b, (((1,), (1,)), ((), ())), precision=HI, preferred_element_type=F32)


def kernel(
    bands, tgt, src_h, order_h, wid_h, lq_h, pw_h, pb_h, kw_h, vm_h, wq_h, wk_h, wv_h, wo_h, gain_h, up_h, upb_h, down_h,
    out,
    src, order, wid, lq, pw, pb, kw, vm, wq, wk, wv, wo, gain, up, upb, down,
    raw, addr_v, addr, ordered, sbuf, gmat, wts, cost,
    st, st_core, st_x, st_h, zc, core_in, zx, x_in, zh, h_in, zt, fin_out, fin_in,
    wsem, tsem, asem, ssem, rsem,
):
    band = lax.axis_index("src")
    t = lax.axis_index("tgt")
    x = t // (NH * NC)
    h = (t // NC) % NH
    c = t % NC
    mine = c * NX + x

    def tid(xx, hh, cc):
        return (xx * NH + hh) * NC + cc

    sib = (band, tid(x, h, 1 - c))
    xs = [(x + d) % NX for d in range(1, NX)]
    hs = [(h + d) % NH for d in range(1, NH)]
    x_peer = [(band, tid(xx, h, c)) for xx in xs]
    h_peer = [(band, tid(x, hh, c)) for hh in hs]
    o_peer = [(band, tid((x + d) % NX, h, 1 - c)) for d in range(1, NX)]
    up_band = (band + 1) % bands
    down_band = (band + bands - 1) % bands
    y_peer = [(up_band, t), (down_band, t)]

    weights = list(zip(
        (src_h, order_h, wid_h, lq_h, pw_h, pb_h, kw_h, vm_h, wq_h, wk_h, wv_h, wo_h, gain_h, up_h, upb_h, down_h),
        (src, order, wid, lq, pw, pb, kw, vm, wq, wk, wv, wo, gain, up, upb, down),
    ))
    loads = [pltpu.make_async_copy(a, b, wsem.at[i]) for i, (a, b) in enumerate(weights)]
    for one in loads[:2]:
        one.start()
    load_target = pltpu.make_async_copy(tgt, raw.at[pl.ds(8, 2 * TARGETS)], tsem)
    load_target.start()
    for one in loads[2:]:
        one.start()

    barrier = pltpu.get_barrier_semaphore()
    partners = [sib] + x_peer + o_peer + h_peer + y_peer
    for who in partners:
        pl.semaphore_signal(barrier, inc=1, device_id=who, device_id_type=MESH)

    loads[0].wait()
    loads[1].wait()
    ids = order[...] & (TARGETS - 1)
    addr_v[...] = (ids >> 3) * 16 + (ids & 7)
    to_smem = pltpu.make_async_copy(addr_v, addr, asem)
    to_smem.start()

    count = [0]
    sends = []

    def send(a, b, who):
        n = count[0]
        count[0] = n + 1
        copy = pltpu.make_async_remote_copy(
            src_ref=a, dst_ref=b, send_sem=ssem.at[n], recv_sem=rsem.at[n], device_id=who, device_id_type=MESH
        )
        copy.start()
        sends.append(copy)
        return copy

    pl.semaphore_wait(barrier, len(partners))

    slot = pl.multiple_of(c * (NX * ROWS) + x * ROWS, ROWS)
    half = pl.multiple_of(c * (NX * ROWS), NX * ROWS)
    sbuf[h, pl.ds(slot, ROWS), :] = src[...] * (1.0 / math.sqrt(C))
    own = sbuf.at[h, pl.ds(slot, ROWS)]
    s1 = [send(own, own, who) for who in h_peer]

    for one in loads[2:]:
        one.wait()
    scale = 1.0 / math.sqrt(D)
    kq = nt(lq[...], kw[...]) * scale
    w2 = nt(kq, pw[...])
    bias_k = jnp.sum(kq * pb[...], axis=1, keepdims=True)
    w2x4 = jnp.concatenate([w2] * 4, axis=1)
    patch_of = lax.broadcasted_iota(jnp.int32, (K, 4 * PATCH), 1) // PATCH
    spread = jnp.concatenate([jnp.where(patch_of == i, w2x4, 0.0) for i in range(4)], axis=0)

    load_target.wait()
    to_smem.wait()
    sub = lax.broadcasted_iota(jnp.int32, (8, 128), 0)
    masks = [sub == i for i in range(8)]

    def gather_patch(p, _):
        for g in range(8):
            at = [addr[p // 2, (p % 2) * 64 + g * 8 + i] for i in range(8)]
            for lane in range(2):
                rows = [raw[pl.ds(at[i] + 8 + 8 * lane - i, 8), :] for i in range(8)]
                total = rows[0]
                for i in range(1, 8):
                    total = jnp.where(masks[i], rows[i], total)
                ordered[p, g, :, lane * 128:lane * 128 + 128] = total
        return 0

    def gather(first, last):
        lax.fori_loop(first, last, gather_patch, 0)

    gather(0, 16)
    for one in s1:
        one.wait_recv()
    col = sbuf.at[:, pl.ds(slot, ROWS)]
    s2 = [send(col, col, who) for who in x_peer]
    gather(16, 40)
    for one in s2:
        one.wait_recv()
    part = sbuf.at[:, pl.ds(half, NX * ROWS)]
    s3 = send(part, part, sib)
    gather(40, 64)

    def score_weights(g, _):
        block = ordered[pl.ds(g * 4, 4)].reshape(4 * PATCH, C)
        gmat[pl.ds(pl.multiple_of(g * 32, 32), 32), :] = nn(spread, block)
        return 0

    lax.fori_loop(0, PATCHES // 4, score_weights, 0)
    s3.wait_recv()

    rows = sbuf[...].reshape(BAND, C)
    score = nt(gmat[...], rows).reshape(PATCHES, K, BAND) + bias_k[None]
    peak = jnp.max(score, axis=0)
    weight = jnp.exp(score - peak[None])
    wts[...] = weight
    st[0] = peak
    st[1] = jnp.sum(weight, axis=0)
    m1 = send(st, st_core, sib)

    def cost_chunk(q, _):
        block = ordered[:, pl.ds(q * 2, 2)].reshape(PATCHES * QC, C)
        cost[q] = nt(block, sbuf[...].reshape(BAND, C)).reshape(PATCHES, QC, BAND)
        return 0

    def join(values):
        top = functools.reduce(jnp.maximum, [a for a, _ in values])
        return top, sum(b * jnp.exp(a - top) for a, b in values)

    lax.fori_loop(0, 1, cost_chunk, 0)
    m1.wait_recv()
    top, tot = join([(peak, st[1]), (st_core[0], st_core[1])])
    st_x[NX - 1, 0] = top
    st_x[NX - 1, 1] = tot
    m2 = [send(st_x.at[NX - 1], st_x.at[i], who) for i, who in enumerate(x_peer)]
    lax.fori_loop(1, 3, cost_chunk, 0)
    for one in m2:
        one.wait_recv()
    top, tot = join([(st_x[i, 0], st_x[i, 1]) for i in range(NX)])
    st_h[NH - 1, 0] = top
    st_h[NH - 1, 1] = tot
    m3 = [send(st_h.at[NH - 1], st_h.at[i], who) for i, who in enumerate(h_peer)]
    lax.fori_loop(3, 4, cost_chunk, 0)

    pv = nn(pw[...], vm[...])
    bv = nn(pb[...], vm[...])
    pk = nn(pv, wk[...])
    bk = nn(bv, wk[...])
    pq = nn(pv, wq[...]) * scale
    bq = nn(bv, wq[...]) * scale
    val = nn(wv[...], wo[...])
    pval = nn(pv, val)
    bval = nn(bv, val)
    pk_all = jnp.concatenate([pk, jnp.broadcast_to(bk, (PATCH, D))], axis=0)
    wq_all = nt(pq, pk_all)
    cq_all = nt(bq, pk_all)

    nat = lax.broadcasted_iota(jnp.int32, (BAND, BAND), 0)
    pos = lax.broadcasted_iota(jnp.int32, (BAND, BAND), 1)
    ph, pc, px, pr = pos // 64, (pos // 32) % 2, (pos // 8) % 4, pos % 8
    perm = jnp.where(nat == px * 64 + ph * 16 + pc * 8 + pr, 1.0, 0.0).astype(F32)
    id_rows = []
    for b in (down_band, band, up_band):
        two = [wid[pl.ds(2 * b + i, 1), :].astype(F32) for i in range(2)]
        id_rows.append(nn(jnp.broadcast_to(jnp.concatenate(two, axis=1), (8, BAND)), perm)[0:1])
    picked = lax.broadcasted_iota(jnp.int32, (PIX, BAND), 1) == lax.broadcasted_iota(jnp.int32, (PIX, BAND), 0) + h * PIX
    q_ids = jnp.sum(jnp.where(picked, id_rows[1], 0.0), axis=1, keepdims=True)
    choose = jnp.where(picked, 1.0, 0.0).astype(F32)

    for one in m3:
        one.wait_recv()
    top, tot = join([(st_h[i, 0], st_h[i, 1]) for i in range(NH)])
    factor = jnp.exp(st[0] - top) / tot

    def chunk_of(i):
        return (h + 1 + i) % NH

    def sums(i):
        q = chunk_of(i)
        for lane in range(2):
            cut = slice(lane * 128, lane * 128 + 128)

            def step(p, acc):
                both = cost[q, p, :, cut]
                new = []
                for k in range(K):
                    w = jnp.broadcast_to(wts[p, k:k + 1, cut], (8, 128))
                    new.append(acc[2 * k] + w * both[0:8])
                    new.append(acc[2 * k + 1] + w * both[8:16])
                return tuple(new)

            acc = lax.fori_loop(0, PATCHES, step, tuple(jnp.zeros((8, 128), F32) for _ in range(2 * K)), unroll=8)
            for k in range(K):
                f = factor[k:k + 1, cut]
                zc[i, k, 0:8, cut] = acc[2 * k] * f
                zc[i, k, 8:16, cut] = acc[2 * k + 1] * f
        return send(zc.at[i, pl.ds((1 - c) * NX, NX)], core_in.at[i], sib)

    def over_x(i, came):
        came.wait_recv()
        zx[i] = zc[i, pl.ds(c * NX, NX)] + core_in[i]
        return [send(zx.at[i, xx], x_in.at[i, j], who) for j, (xx, who) in enumerate(zip(xs, x_peer))]

    def over_h(i, came):
        for one in came:
            one.wait_recv()
        zh[i] = zx[i, x] + x_in[i, 0] + x_in[i, 1] + x_in[i, 2]
        if i < NH - 1:
            return send(zh.at[i], h_in.at[i], h_peer[i])

    a0 = sums(0)
    a1 = sums(1)
    b0 = over_x(0, a0)
    a2 = sums(2)
    b1 = over_x(1, a1)
    d0 = over_h(0, b0)
    a3 = sums(3)
    b2 = over_x(2, a2)
    d1 = over_h(1, b1)
    b3 = over_x(3, a3)
    d2 = over_h(2, b2)
    over_h(3, b3)
    for one in (d0, d1, d2):
        one.wait_recv()
    q_rows = pl.ds(pl.multiple_of(h * QC, QC), QC)
    zt[1, q_rows, :] = zh[NH - 1] + h_in[0] + h_in[1] + h_in[2]

    def to_bands(rows):
        return [send(zt.at[1, rows], zt.at[0, rows], y_peer[0]), send(zt.at[1, rows], zt.at[2, rows], y_peer[1])]

    e = [send(zt.at[1, q_rows], zt.at[1, q_rows], who) for who in h_peer]
    f = to_bands(q_rows)
    for d in range(1, NH):
        e[d - 1].wait_recv()
        f += to_bands(pl.ds(pl.multiple_of(((h + NH - d) % NH) * QC, QC), QC))

    zq = nt(choose, zt[1])
    qa = nn(zq, wq_all) + cq_all
    qz = qa[:, 0:PATCH]
    qb = qa[:, PATCH:PATCH + 1]
    for one in f:
        one.wait_recv()
    logits = jnp.concatenate([nn(qz, zt[b]) for b in range(3)], axis=1) + qb
    same = q_ids == jnp.concatenate(id_rows, axis=1)
    logits = jnp.where(same, logits, -jnp.inf)
    attend = jnp.exp(logits - jnp.max(logits, axis=1, keepdims=True))
    attend = attend / jnp.sum(attend, axis=1, keepdims=True)
    zmix = sum(nt(attend[:, b * BAND:(b + 1) * BAND], zt[b]) for b in range(3))
    resid = (nn(zq, pv) + bv) + (nn(zmix, pval) + bval)
    center = jnp.mean(resid, axis=-1, keepdims=True)
    var = jnp.mean((resid - center) ** 2, axis=-1, keepdims=True)
    normed = (resid - center) / jnp.sqrt(var + 1e-05) * gain[...]
    hidden = jax.nn.gelu(nn(normed, up[...]) + upb[...])
    fin_out[...] = resid + nn(hidden, down[...])

    g = []
    for d in range(1, NX):
        rows = pl.ds(pl.multiple_of((c * NX + xs[d - 1]) * ROWS, ROWS), ROWS)
        g.append(send(fin_out.at[rows], fin_in.at[mine], x_peer[d - 1]))
    for d in range(NX):
        rows = pl.ds(pl.multiple_of(((1 - c) * NX + (x + d) % NX) * ROWS, ROWS), ROWS)
        g.append(send(fin_out.at[rows], fin_in.at[mine], sib if d == 0 else o_peer[d - 1]))
    fin_in[mine] = fin_out[pl.ds(pl.multiple_of(mine * ROWS, ROWS), ROWS)]
    for one in g:
        one.wait_recv()
    for k in range(K):
        out[:, k, :] = fin_in[k]
    for one in sends:
        one.wait_send()


COPIES = 90


def local(
    source_feat, target_feat, target_order, window_id, latent_query, patch_weight, patch_embed_bias, key_weight,
    value_matrix, window_query, window_key, window_value, window_out, norm_gain, up_weight, up_bias, down_weight,
):
    bands = lax.axis_size("src")
    tiles = target_feat.reshape(TARGETS // 8, 8, 2, 128).transpose(0, 2, 1, 3).reshape(2 * TARGETS, 128)
    params = (
        source_feat, target_order.reshape(32, 128), window_id.reshape(16, 128),
        latent_query, patch_weight, patch_embed_bias.reshape(1, -1), key_weight, value_matrix, window_query, window_key,
        window_value, window_out, norm_gain.reshape(1, -1), up_weight, up_bias.reshape(1, -1), down_weight,
    )
    vmem = pl.BlockSpec(memory_space=pltpu.VMEM)
    hbm = pl.BlockSpec(memory_space=pl.ANY)
    scratch = [pltpu.VMEM(p.shape, p.dtype) for p in params]
    scratch += [
        pltpu.VMEM((2 * TARGETS + 16, 128), F32),
        pltpu.VMEM((32, 128), jnp.int32),
        pltpu.SMEM((32, 128), jnp.int32),
        pltpu.VMEM((PATCHES, 8, 8, C), F32),
        pltpu.VMEM((NH, PIX, C), F32),
        pltpu.VMEM((PATCHES * K, C), F32),
        pltpu.VMEM((PATCHES, K, BAND), F32),
        pltpu.VMEM((NH, PATCHES, QC, BAND), F32),
        pltpu.VMEM((2, K, BAND), F32),
        pltpu.VMEM((2, K, BAND), F32),
        pltpu.VMEM((NX, 2, K, BAND), F32),
        pltpu.VMEM((NH, 2, K, BAND), F32),
        pltpu.VMEM((NH, K, QC, BAND), F32),
        pltpu.VMEM((NH, NX, QC, BAND), F32),
        pltpu.VMEM((NH, NX, QC, BAND), F32),
        pltpu.VMEM((NH, NX - 1, QC, BAND), F32),
        pltpu.VMEM((NH, QC, BAND), F32),
        pltpu.VMEM((NH - 1, QC, BAND), F32),
        pltpu.VMEM((3, PATCH, BAND), F32),
        pltpu.VMEM((PIX, D), F32),
        pltpu.VMEM((K, ROWS, D), F32),
        pltpu.SemaphoreType.DMA((len(params),)),
        pltpu.SemaphoreType.DMA,
        pltpu.SemaphoreType.DMA,
        pltpu.SemaphoreType.DMA((COPIES,)),
        pltpu.SemaphoreType.DMA((COPIES,)),
    ]
    return pl.pallas_call(
        functools.partial(kernel, bands),
        out_shape=jax.ShapeDtypeStruct((ROWS, K, D), F32),
        in_specs=[hbm] * (1 + len(params)),
        out_specs=vmem,
        scratch_shapes=scratch,
        compiler_params=pltpu.CompilerParams(
            collective_id=0, has_side_effects=True, vmem_limit_bytes=60 * 1024 * 1024
        ),
        name="encode",
    )(tiles, *params)


def solution(mesh):
    placed = (P(("src", "tgt"), None), P("tgt", None), P("tgt")) + (P(),) * 14
    return jax.shard_map(
        local, mesh=mesh, in_specs=placed, out_specs=P(("src", "tgt"), None, None), check_vma=False
    )
```

time: 501 us -> 68.3 us (0.14)
  waiting for transfers between devices: 140 us -> 0 us
  blocking collectives: 135 us -> 0 us
  local copies, waits for them, and re-layouts: 73.6 us -> 1.38 us
  other arithmetic: 69.9 us -> 0 us
  Pallas kernels: 0 us -> 66.7 us
  matrix products: 55.9 us -> 0 us
  between operations: 14 us -> 0.01 us
  starting transfers between devices: 6.33 us -> 0 us
    all_gather x3 -> x0, blocking collectives: 135 us -> none  [the longest x2 85.2 us: merged(): pieces = jax.tree.map(lambda part: lax.all_gather(part, axis), value)]
    all_gather x1 -> x0, waiting for transfers between devices: 116 us -> none  [merged(): pieces = jax.tree.map(lambda part: lax.all_gather(part, axis), value)]
    add x63 -> x0, other arithmetic: 67.5 us -> none  [the longest x31 66.9 us: combine_softmax(): return (peak, total, (part_one + part_two).reshape(row_count, -1))]
    pallas_call x0 -> x1, Pallas kernels: none -> 66.7 us  [local(): pl.pallas_call(functools.partial(kernel, bands), out_shape=jax.ShapeDtype...]
    dot_general x14 -> x0, matrix products: 55.9 us -> none  [the longest x1 14.8 us: partial_block(): jnp.einsum('bkp,bpx->bkx', weights, source, precision=HIGH_PRECISION)]
    ppermute x2 -> x0, waiting for transfers between devices: 24.1 us -> none  [passed_along(): return lax.ppermute(block, axis, route)]
    slice x5 -> x0, local copies, waits for them, and re-layouts: 23 us -> none  [the longest x3 23 us: merged(): tail = jax.tree.map(lambda part: part[1:], pieces)]
    mul x62 -> x0, local copies, waits for them, and re-layouts: 20.8 us -> none  [the longest x31 10.4 us: combine_softmax(): summed_two.reshape(row_count, latents, -1) * factor_two[:, :, None]]
  transfers between devices with their start and end apart: 3 -> 0, of which waited for: 3 -> 0; matrix products, arithmetic and copies ran while one was open for 0% -> 0% of each run, Pallas kernels for 0% -> 0%
where the time goes in v1:
time: 68.3 us; the launch traced here: 68.1 us
  Pallas kernels  66.7 us (98%)
  local copies, waits for them, and re-layouts  1.38 us (2%)
    pallas_call x1, Pallas kernels, local(): pl.pallas_call(functools.partial(kernel, bands), out_shape=jax.ShapeDtype...  66.7 us
    unnamed x1, local copies, waits for them, and re-layouts  1.38 us

profile of v1, /device:TPU:1, one launch (start us, length us, event | category | flops | bytes accessed | tf_op | source)
XLA Modules:
  0.0 68.1 jit_solution(9665675676364574910)
XLA Ops:
  0.0 66.7 %encode.1 = f32[8,8,128]{2,1,0:T(8,128)} custom-call(f32[8192,128]{1,0:T(8,128)} %bitcast.10, f32[8,256]{1,0:T(8,128)} %src_h.1, s32[32,128]{1,0:T(8,128)} %bitcast.11, s32[16,128]{1,0:T(8,128)} %bitcast.12, f32[8,128]{1,0:T(8,128)} %lq_h.1, f32[64,128]{1,0:T(8,128)} %pw_h.1, f32[1,128]{1,0:T(1,128)} %bitcast.14, f32[128,128]{1,0:T(8,128)} %kw_h.1, ...), custom_call_target="tpu_custom_call" | custom-call | tf_op jit(solution)/shard_map/encode/pallas_call | solution.py:363
  66.8 1.4 %copy.19 = f32[8,8,128]{2,1,0:T(8,128)} copy(f32[8,8,128]{2,1,0:T(8,128)} %encode.1) | data formatting | bytes 65536

commit v2 on v1

--- a/solution.py
+++ b/solution.py
@@ -21,12 +21,22 @@
 TARGETS = 4096
 PATCHES = TARGETS // PATCH
 ROWS = 8
-QC = PATCH // NH
+PARTS = 4
+QC = PATCH // PARTS
 PIX = BAND // NH
 
 
 def nn(a, b):
     return lax.dot_general(a, b, (((1,), (0,)), ((), ())), precision=HI, preferred_element_type=F32)
+
+
+def nt16(a, b):
+    return lax.dot_general(a, b, (((1,), (1,)), ((), ())), preferred_element_type=F32)
+
+
+def halves(a):
+    high = a.astype(jnp.bfloat16)
+    return high, (a - high.astype(F32)).astype(jnp.bfloat16)
 
 
 def nt(a, b):
@@ -37,8 +47,8 @@
     bands, tgt, src_h, order_h, wid_h, lq_h, pw_h, pb_h, kw_h, vm_h, wq_h, wk_h, wv_h, wo_h, gain_h, up_h, upb_h, down_h,
     out,
     src, order, wid, lq, pw, pb, kw, vm, wq, wk, wv, wo, gain, up, upb, down,
-    raw, addr_v, addr, ordered, sbuf, gmat, wts, cost,
-    st, st_core, st_x, st_h, zc, core_in, zx, x_in, zh, h_in, zt, fin_out, fin_in,
+    raw, addr_v, addr, ordered, sbuf, scat, gmat, wts, cost,
+    st, st_core, fac, st_x, st_h, zc, core_in, zx, x_in, zh, h_in, zt, fin_out, fin_in,
     wsem, tsem, asem, ssem, rsem,
 ):
     band = lax.axis_index("src")
@@ -74,7 +84,7 @@
         one.start()
 
     barrier = pltpu.get_barrier_semaphore()
-    partners = [sib] + x_peer + o_peer + h_peer + y_peer
+    partners = h_peer + y_peer + x_peer + o_peer + [sib]
     for who in partners:
         pl.semaphore_signal(barrier, inc=1, device_id=who, device_id_type=MESH)
 
@@ -98,14 +108,40 @@
         sends.append(copy)
         return copy
 
-    pl.semaphore_wait(barrier, len(partners))
-
     slot = pl.multiple_of(c * (NX * ROWS) + x * ROWS, ROWS)
     half = pl.multiple_of(c * (NX * ROWS), NX * ROWS)
     sbuf[h, pl.ds(slot, ROWS), :] = src[...] * (1.0 / math.sqrt(C))
+    pl.semaphore_wait(barrier, len(partners))
     own = sbuf.at[h, pl.ds(slot, ROWS)]
     s1 = [send(own, own, who) for who in h_peer]
 
+    load_target.wait()
+    to_smem.wait()
+    sub = lax.broadcasted_iota(jnp.int32, (8, 128), 0)
+    masks = [sub == i for i in range(8)]
+
+    def gather_pair(r, _):
+        for g in range(16):
+            p = 2 * r + g // 8
+            at = [addr[r, g * 8 + i] for i in range(8)]
+            for lane in range(2):
+                cols = slice(lane * 128, lane * 128 + 128)
+                rows = [raw[pl.ds(at[i] + 8 + 8 * lane - i, 8), :] for i in range(8)]
+                total = rows[0]
+                for i in range(1, 8):
+                    total = jnp.where(masks[i], rows[i], total)
+                ordered[p, g % 8, :, cols] = total
+        return 0
+
+    def gather(first, last):
+        lax.fori_loop(first, last, gather_pair, 0)
+
+    gather(0, 20)
+    for one in s1:
+        one.wait_recv()
+    col = sbuf.at[:, pl.ds(slot, ROWS)]
+    s2 = [send(col, col, who) for who in x_peer]
+    gather(20, 32)
     for one in loads[2:]:
         one.wait()
     scale = 1.0 / math.sqrt(D)
@@ -116,78 +152,96 @@
     patch_of = lax.broadcasted_iota(jnp.int32, (K, 4 * PATCH), 1) // PATCH
     spread = jnp.concatenate([jnp.where(patch_of == i, w2x4, 0.0) for i in range(4)], axis=0)
 
-    load_target.wait()
-    to_smem.wait()
-    sub = lax.broadcasted_iota(jnp.int32, (8, 128), 0)
-    masks = [sub == i for i in range(8)]
-
-    def gather_patch(p, _):
-        for g in range(8):
-            at = [addr[p // 2, (p % 2) * 64 + g * 8 + i] for i in range(8)]
-            for lane in range(2):
-                rows = [raw[pl.ds(at[i] + 8 + 8 * lane - i, 8), :] for i in range(8)]
-                total = rows[0]
-                for i in range(1, 8):
-                    total = jnp.where(masks[i], rows[i], total)
-                ordered[p, g, :, lane * 128:lane * 128 + 128] = total
-        return 0
-
-    def gather(first, last):
-        lax.fori_loop(first, last, gather_patch, 0)
-
-    gather(0, 16)
-    for one in s1:
-        one.wait_recv()
-    col = sbuf.at[:, pl.ds(slot, ROWS)]
-    s2 = [send(col, col, who) for who in x_peer]
-    gather(16, 40)
-    for one in s2:
-        one.wait_recv()
-    part = sbuf.at[:, pl.ds(half, NX * ROWS)]
-    s3 = send(part, part, sib)
-    gather(40, 64)
 
     def score_weights(g, _):
         block = ordered[pl.ds(g * 4, 4)].reshape(4 * PATCH, C)
         gmat[pl.ds(pl.multiple_of(g * 32, 32), 32), :] = nn(spread, block)
         return 0
 
-    lax.fori_loop(0, PATCHES // 4, score_weights, 0)
+    lax.fori_loop(0, PATCHES // 4, score_weights, 0, unroll=True)
+    for one in s2:
+        one.wait_recv()
+    part = sbuf.at[:, pl.ds(half, NX * ROWS)]
+    s3 = send(part, part, sib)
     s3.wait_recv()
 
-    rows = sbuf[...].reshape(BAND, C)
-    score = nt(gmat[...], rows).reshape(PATCHES, K, BAND) + bias_k[None]
+    score = nt(gmat[...], sbuf[...].reshape(BAND, C)).reshape(PATCHES, K, BAND) + bias_k[None]
     peak = jnp.max(score, axis=0)
     weight = jnp.exp(score - peak[None])
     wts[...] = weight
+    total = jnp.sum(weight, axis=0)
     st[0] = peak
-    st[1] = jnp.sum(weight, axis=0)
+    st[1] = total
     m1 = send(st, st_core, sib)
 
+    shigh, slow = halves(sbuf[...].reshape(BAND, C))
+    scat[:, 0:C] = shigh
+    scat[:, C:2 * C] = slow
+    scat[:, 2 * C:3 * C] = shigh
+
     def cost_chunk(q, _):
-        block = ordered[:, pl.ds(q * 2, 2)].reshape(PATCHES * QC, C)
-        cost[q] = nt(block, sbuf[...].reshape(BAND, C)).reshape(PATCHES, QC, BAND)
+        block = ordered[:, pl.ds(q * (QC // 8), QC // 8)].reshape(PATCHES * QC, C)
+        a, b = halves(block)
+        part = nt16(jnp.concatenate([a, a, b], axis=1), scat[...])
+        cost[q] = part.reshape(PATCHES, QC, BAND)
         return 0
 
     def join(values):
         top = functools.reduce(jnp.maximum, [a for a, _ in values])
-        return top, sum(b * jnp.exp(a - top) for a, b in values)
-
-    lax.fori_loop(0, 1, cost_chunk, 0)
+        scales = [jnp.exp(a - top) for a, _ in values]
+        return top, sum(b * f for (_, b), f in zip(values, scales)), scales
+
+    lax.fori_loop(0, PARTS, cost_chunk, 0)
     m1.wait_recv()
-    top, tot = join([(peak, st[1]), (st_core[0], st_core[1])])
-    st_x[NX - 1, 0] = top
-    st_x[NX - 1, 1] = tot
-    m2 = [send(st_x.at[NX - 1], st_x.at[i], who) for i, who in enumerate(x_peer)]
-    lax.fori_loop(1, 3, cost_chunk, 0)
-    for one in m2:
-        one.wait_recv()
-    top, tot = join([(st_x[i, 0], st_x[i, 1]) for i in range(NX)])
-    st_h[NH - 1, 0] = top
-    st_h[NH - 1, 1] = tot
-    m3 = [send(st_h.at[NH - 1], st_h.at[i], who) for i, who in enumerate(h_peer)]
-    lax.fori_loop(3, 4, cost_chunk, 0)
-
+    top, tot, scales = join([(st[0], st[1]), (st_core[0], st_core[1])])
+    fac[0] = scales[0]
+    fac[1] = scales[1]
+    for k in range(K):
+        st_x[k, 0:1, :] = top[k:k + 1]
+        st_x[k, 1:2, :] = tot[k:k + 1]
+    m2 = [send(st_x.at[c * NX + xx], st_x.at[K + i], who) for i, (xx, who) in enumerate(zip(xs, x_peer))]
+
+    def sums(i):
+        for lane in range(2):
+            cols = slice(lane * 128, lane * 128 + 128)
+
+            def step(p, acc):
+                rows = [cost[i, p, g * 8:g * 8 + 8, cols] for g in range(QC // 8)]
+                new = []
+                for k in range(K):
+                    w = jnp.broadcast_to(wts[p, k:k + 1, cols], (8, 128))
+                    new.extend(acc[k * len(rows) + g] + w * one for g, one in enumerate(rows))
+                return tuple(new)
+
+            zero = tuple(jnp.zeros((8, 128), F32) for _ in range(QC // 8 * K))
+            acc = lax.fori_loop(0, PATCHES, step, zero, unroll=8)
+            for k in range(K):
+                for g in range(QC // 8):
+                    zc[i, k, g * 8:g * 8 + 8, cols] = acc[k * (QC // 8) + g]
+        return send(zc.at[i, pl.ds((1 - c) * NX, NX)], core_in.at[i], sib)
+
+    def over_x(i, came):
+        came.wait_recv()
+        for j in range(NX):
+            k = c * NX + j
+            zx[i, j] = zc[i, k] * fac[0, pl.ds(k, 1), :] + core_in[i, j] * fac[1, pl.ds(k, 1), :]
+        return [send(zx.at[i, xx], x_in.at[i, j], who) for j, (xx, who) in enumerate(zip(xs, x_peer))]
+
+    def x_stats():
+        for one in m2:
+            one.wait_recv()
+        top, tot, scales = join([(st_x[i, 0:1, :], st_x[i, 1:2, :]) for i in (mine, K, K + 1, K + 2)])
+        st_h[0, 0:1, :] = top
+        st_h[0, 1:2, :] = tot
+        return [send(st_h.at[0], st_h.at[1 + i], who) for i, who in enumerate(h_peer)], scales
+
+    core = [sums(0)]
+    over = []
+    for i in range(1, PARTS):
+        core.append(sums(i))
+        over.append(over_x(i - 1, core[i - 1]))
+    over.append(over_x(PARTS - 1, core[PARTS - 1]))
+    m3, x_scales = x_stats()
     pv = nn(pw[...], vm[...])
     bv = nn(pb[...], vm[...])
     pk = nn(pv, wk[...])
@@ -213,72 +267,35 @@
     q_ids = jnp.sum(jnp.where(picked, id_rows[1], 0.0), axis=1, keepdims=True)
     choose = jnp.where(picked, 1.0, 0.0).astype(F32)
 
-    for one in m3:
-        one.wait_recv()
-    top, tot = join([(st_h[i, 0], st_h[i, 1]) for i in range(NH)])
-    factor = jnp.exp(st[0] - top) / tot
-
-    def chunk_of(i):
-        return (h + 1 + i) % NH
-
-    def sums(i):
-        q = chunk_of(i)
-        for lane in range(2):
-            cut = slice(lane * 128, lane * 128 + 128)
-
-            def step(p, acc):
-                both = cost[q, p, :, cut]
-                new = []
-                for k in range(K):
-                    w = jnp.broadcast_to(wts[p, k:k + 1, cut], (8, 128))
-                    new.append(acc[2 * k] + w * both[0:8])
-                    new.append(acc[2 * k + 1] + w * both[8:16])
-                return tuple(new)
-
-            acc = lax.fori_loop(0, PATCHES, step, tuple(jnp.zeros((8, 128), F32) for _ in range(2 * K)), unroll=8)
-            for k in range(K):
-                f = factor[k:k + 1, cut]
-                zc[i, k, 0:8, cut] = acc[2 * k] * f
-                zc[i, k, 8:16, cut] = acc[2 * k + 1] * f
-        return send(zc.at[i, pl.ds((1 - c) * NX, NX)], core_in.at[i], sib)
-
-    def over_x(i, came):
-        came.wait_recv()
-        zx[i] = zc[i, pl.ds(c * NX, NX)] + core_in[i]
-        return [send(zx.at[i, xx], x_in.at[i, j], who) for j, (xx, who) in enumerate(zip(xs, x_peer))]
 
     def over_h(i, came):
         for one in came:
             one.wait_recv()
-        zh[i] = zx[i, x] + x_in[i, 0] + x_in[i, 1] + x_in[i, 2]
-        if i < NH - 1:
-            return send(zh.at[i], h_in.at[i], h_peer[i])
-
-    a0 = sums(0)
-    a1 = sums(1)
-    b0 = over_x(0, a0)
-    a2 = sums(2)
-    b1 = over_x(1, a1)
-    d0 = over_h(0, b0)
-    a3 = sums(3)
-    b2 = over_x(2, a2)
-    d1 = over_h(1, b1)
-    b3 = over_x(3, a3)
-    d2 = over_h(2, b2)
-    over_h(3, b3)
-    for one in (d0, d1, d2):
-        one.wait_recv()
-    q_rows = pl.ds(pl.multiple_of(h * QC, QC), QC)
-    zt[1, q_rows, :] = zh[NH - 1] + h_in[0] + h_in[1] + h_in[2]
-
-    def to_bands(rows):
-        return [send(zt.at[1, rows], zt.at[0, rows], y_peer[0]), send(zt.at[1, rows], zt.at[2, rows], y_peer[1])]
-
-    e = [send(zt.at[1, q_rows], zt.at[1, q_rows], who) for who in h_peer]
-    f = to_bands(q_rows)
-    for d in range(1, NH):
-        e[d - 1].wait_recv()
-        f += to_bands(pl.ds(pl.multiple_of(((h + NH - d) % NH) * QC, QC), QC))
+        total = zx[i, x] * x_scales[0]
+        for j in range(NX - 1):
+            total = total + x_in[i, j] * x_scales[1 + j]
+        zh[i] = total
+        return [send(zh.at[i], h_in.at[i, j], who) for j, who in enumerate(h_peer)]
+
+    d = [over_h(i, came) for i, came in enumerate(over)]
+    for one in m3:
+        one.wait_recv()
+    _, tot, h_scales = join([(st_h[i, 0:1, :], st_h[i, 1:2, :]) for i in range(NH)])
+    inverse = 1.0 / tot
+    h_scales = [f * inverse for f in h_scales]
+
+    def to_bands(i):
+        for one in d[i]:
+            one.wait_recv()
+        total = zh[i] * h_scales[0]
+        for j in range(NH - 1):
+            total = total + h_in[i, j] * h_scales[1 + j]
+        rows = slice(i * QC, (i + 1) * QC)
+        zt[1, rows, :] = total
+        part = zt.at[1, pl.ds(i * QC, QC)]
+        return [send(part, zt.at[b, pl.ds(i * QC, QC)], who) for b, who in zip((0, 2), y_peer)]
+
+    f = [one for i in range(PARTS) for one in to_bands(i)]
 
     zq = nt(choose, zt[1])
     qa = nn(zq, wq_all) + cq_all
@@ -338,19 +355,21 @@
         pltpu.SMEM((32, 128), jnp.int32),
         pltpu.VMEM((PATCHES, 8, 8, C), F32),
         pltpu.VMEM((NH, PIX, C), F32),
+        pltpu.VMEM((BAND, 3 * C), jnp.bfloat16),
         pltpu.VMEM((PATCHES * K, C), F32),
         pltpu.VMEM((PATCHES, K, BAND), F32),
-        pltpu.VMEM((NH, PATCHES, QC, BAND), F32),
+        pltpu.VMEM((PARTS, PATCHES, QC, BAND), F32),
         pltpu.VMEM((2, K, BAND), F32),
         pltpu.VMEM((2, K, BAND), F32),
-        pltpu.VMEM((NX, 2, K, BAND), F32),
-        pltpu.VMEM((NH, 2, K, BAND), F32),
-        pltpu.VMEM((NH, K, QC, BAND), F32),
-        pltpu.VMEM((NH, NX, QC, BAND), F32),
-        pltpu.VMEM((NH, NX, QC, BAND), F32),
-        pltpu.VMEM((NH, NX - 1, QC, BAND), F32),
-        pltpu.VMEM((NH, QC, BAND), F32),
-        pltpu.VMEM((NH - 1, QC, BAND), F32),
+        pltpu.VMEM((2, K, BAND), F32),
+        pltpu.VMEM((K + NX - 1, 8, BAND), F32),
+        pltpu.VMEM((NH, 8, BAND), F32),
+        pltpu.VMEM((PARTS, K, QC, BAND), F32),
+        pltpu.VMEM((PARTS, NX, QC, BAND), F32),
+        pltpu.VMEM((PARTS, NX, QC, BAND), F32),
+        pltpu.VMEM((PARTS, NX - 1, QC, BAND), F32),
+        pltpu.VMEM((PARTS, QC, BAND), F32),
+        pltpu.VMEM((PARTS, NH - 1, QC, BAND), F32),
         pltpu.VMEM((3, PATCH, BAND), F32),
         pltpu.VMEM((PIX, D), F32),
         pltpu.VMEM((K, ROWS, D), F32),

time: 68.3 us -> 52 us (0.76)
  Pallas kernels: 66.7 us -> 50.5 us
    pallas_call x1, Pallas kernels: 66.7 us -> 50.5 us  [local(): pl.pallas_call(functools.partial(kernel, bands), out_shape=jax.ShapeDtype...]
where the time goes in v2:
time: 52 us; the launch traced here: 51.9 us
  Pallas kernels  50.5 us (97%)
  local copies, waits for them, and re-layouts  1.38 us (3%)
    pallas_call x1, Pallas kernels, local(): pl.pallas_call(functools.partial(kernel, bands), out_shape=jax.ShapeDtype...  50.5 us
    unnamed x1, local copies, waits for them, and re-layouts  1.38 us

profile of v2, /device:TPU:1, one launch (start us, length us, event | category | flops | bytes accessed | tf_op | source)
XLA Modules:
  0.0 51.9 jit_solution(9839055563286593204)
XLA Ops:
  0.0 50.5 %encode.1 = f32[8,8,128]{2,1,0:T(8,128)} custom-call(f32[8192,128]{1,0:T(8,128)} %bitcast.10, f32[8,256]{1,0:T(8,128)} %src_h.1, s32[32,128]{1,0:T(8,128)} %bitcast.11, s32[16,128]{1,0:T(8,128)} %bitcast.12, f32[8,128]{1,0:T(8,128)} %lq_h.1, f32[64,128]{1,0:T(8,128)} %pw_h.1, f32[1,128]{1,0:T(1,128)} %bitcast.14, f32[128,128]{1,0:T(8,128)} %kw_h.1, ...), custom_call_target="tpu_custom_call" | custom-call | tf_op jit(solution)/shard_map/encode/pallas_call | solution.py:382
  50.5 1.4 %copy.19 = f32[8,8,128]{2,1,0:T(8,128)} copy(f32[8,8,128]{2,1,0:T(8,128)} %encode.1) | data formatting | bytes 65536

commit v3 on v2

--- a/solution.py
+++ b/solution.py
@@ -23,6 +23,7 @@
 ROWS = 8
 PARTS = 4
 QC = PATCH // PARTS
+SHRINK = 1.0 / math.sqrt(C)
 PIX = BAND // NH
 
 
@@ -39,6 +40,12 @@
     return high, (a - high.astype(F32)).astype(jnp.bfloat16)
 
 
+def nn3(a, cat):
+    high, low = halves(a)
+    three = jnp.concatenate([high, high, low], axis=1)
+    return lax.dot_general(three, cat, (((1,), (0,)), ((), ())), preferred_element_type=F32)
+
+
 def nt(a, b):
     return lax.dot_general(a, b, (((1,), (1,)), ((), ())), precision=HI, preferred_element_type=F32)
 
@@ -46,10 +53,10 @@
 def kernel(
     bands, tgt, src_h, order_h, wid_h, lq_h, pw_h, pb_h, kw_h, vm_h, wq_h, wk_h, wv_h, wo_h, gain_h, up_h, upb_h, down_h,
     out,
-    src, order, wid, lq, pw, pb, kw, vm, wq, wk, wv, wo, gain, up, upb, down,
+    order, wid, lq, pw, pb, kw, vm, wq, wk, wv, wo, gain, up, upb, down,
     raw, addr_v, addr, ordered, sbuf, scat, gmat, wts, cost,
-    st, st_core, fac, st_x, st_h, zc, core_in, zx, x_in, zh, h_in, zt, fin_out, fin_in,
-    wsem, tsem, asem, ssem, rsem,
+    st, st_core, fac, st_x, st_h, zc, core_in, zx, x_in, zh, h_in, zt, up_cat, down_cat, fin_out, fin_in,
+    wsem, tsem, asem, ksem, ssem, rsem,
 ):
     band = lax.axis_index("src")
     t = lax.axis_index("tgt")
@@ -72,28 +79,22 @@
     y_peer = [(up_band, t), (down_band, t)]
 
     weights = list(zip(
-        (src_h, order_h, wid_h, lq_h, pw_h, pb_h, kw_h, vm_h, wq_h, wk_h, wv_h, wo_h, gain_h, up_h, upb_h, down_h),
-        (src, order, wid, lq, pw, pb, kw, vm, wq, wk, wv, wo, gain, up, upb, down),
+        (order_h, wid_h, lq_h, pw_h, pb_h, kw_h, vm_h, wq_h, wk_h, wv_h, wo_h, gain_h, up_h, upb_h, down_h),
+        (order, wid, lq, pw, pb, kw, vm, wq, wk, wv, wo, gain, up, upb, down),
     ))
-    loads = [pltpu.make_async_copy(a, b, wsem.at[i]) for i, (a, b) in enumerate(weights)]
-    for one in loads[:2]:
-        one.start()
-    load_target = pltpu.make_async_copy(tgt, raw.at[pl.ds(8, 2 * TARGETS)], tsem)
-    load_target.start()
-    for one in loads[2:]:
-        one.start()
-
     barrier = pltpu.get_barrier_semaphore()
     partners = h_peer + y_peer + x_peer + o_peer + [sib]
     for who in partners:
         pl.semaphore_signal(barrier, inc=1, device_id=who, device_id_type=MESH)
-
-    loads[0].wait()
-    loads[1].wait()
-    ids = order[...] & (TARGETS - 1)
-    addr_v[...] = (ids >> 3) * 16 + (ids & 7)
-    to_smem = pltpu.make_async_copy(addr_v, addr, asem)
-    to_smem.start()
+    loads = [pltpu.make_async_copy(a, b, wsem.at[i]) for i, (a, b) in enumerate(weights)]
+    loads[0].start()
+    load_target = pltpu.make_async_copy(tgt, raw.at[pl.ds(8, 2 * TARGETS)], tsem)
+    load_target.start()
+    slot = pl.multiple_of(c * (NX * ROWS) + x * ROWS, ROWS)
+    half = pl.multiple_of(c * (NX * ROWS), NX * ROWS)
+    own = sbuf.at[h, pl.ds(slot, ROWS)]
+    keep = pltpu.make_async_copy(src_h, own, ksem)
+    keep.start()
 
     count = [0]
     sends = []
@@ -108,13 +109,16 @@
         sends.append(copy)
         return copy
 
-    slot = pl.multiple_of(c * (NX * ROWS) + x * ROWS, ROWS)
-    half = pl.multiple_of(c * (NX * ROWS), NX * ROWS)
-    sbuf[h, pl.ds(slot, ROWS), :] = src[...] * (1.0 / math.sqrt(C))
     pl.semaphore_wait(barrier, len(partners))
-    own = sbuf.at[h, pl.ds(slot, ROWS)]
-    s1 = [send(own, own, who) for who in h_peer]
-
+    s1 = [send(src_h, own, who) for who in h_peer]
+    for one in loads[1:]:
+        one.start()
+
+    loads[0].wait()
+    ids = order[...] & (TARGETS - 1)
+    addr_v[...] = (ids >> 3) * 16 + (ids & 7)
+    to_smem = pltpu.make_async_copy(addr_v, addr, asem)
+    to_smem.start()
     load_target.wait()
     to_smem.wait()
     sub = lax.broadcasted_iota(jnp.int32, (8, 128), 0)
@@ -133,25 +137,21 @@
                 ordered[p, g % 8, :, cols] = total
         return 0
 
-    def gather(first, last):
-        lax.fori_loop(first, last, gather_pair, 0)
-
-    gather(0, 20)
-    for one in s1:
-        one.wait_recv()
-    col = sbuf.at[:, pl.ds(slot, ROWS)]
-    s2 = [send(col, col, who) for who in x_peer]
-    gather(20, 32)
-    for one in loads[2:]:
+    lax.fori_loop(0, PATCHES // 2, gather_pair, 0)
+    for one in loads[1:]:
         one.wait()
     scale = 1.0 / math.sqrt(D)
     kq = nt(lq[...], kw[...]) * scale
-    w2 = nt(kq, pw[...])
+    w2 = nt(kq, pw[...]) * SHRINK
     bias_k = jnp.sum(kq * pb[...], axis=1, keepdims=True)
     w2x4 = jnp.concatenate([w2] * 4, axis=1)
     patch_of = lax.broadcasted_iota(jnp.int32, (K, 4 * PATCH), 1) // PATCH
     spread = jnp.concatenate([jnp.where(patch_of == i, w2x4, 0.0) for i in range(4)], axis=0)
-
+    for one in s1:
+        one.wait_recv()
+    keep.wait()
+    col = sbuf.at[:, pl.ds(slot, ROWS)]
+    s2 = [send(col, col, who) for who in x_peer + o_peer + [sib]]
 
     def score_weights(g, _):
         block = ordered[pl.ds(g * 4, 4)].reshape(4 * PATCH, C)
@@ -161,9 +161,6 @@
     lax.fori_loop(0, PATCHES // 4, score_weights, 0, unroll=True)
     for one in s2:
         one.wait_recv()
-    part = sbuf.at[:, pl.ds(half, NX * ROWS)]
-    s3 = send(part, part, sib)
-    s3.wait_recv()
 
     score = nt(gmat[...], sbuf[...].reshape(BAND, C)).reshape(PATCHES, K, BAND) + bias_k[None]
     peak = jnp.max(score, axis=0)
@@ -174,24 +171,23 @@
     st[1] = total
     m1 = send(st, st_core, sib)
 
-    shigh, slow = halves(sbuf[...].reshape(BAND, C))
+    shigh, slow = halves(sbuf[...].reshape(BAND, C) * SHRINK)
     scat[:, 0:C] = shigh
     scat[:, C:2 * C] = slow
     scat[:, 2 * C:3 * C] = shigh
 
-    def cost_chunk(q, _):
-        block = ordered[:, pl.ds(q * (QC // 8), QC // 8)].reshape(PATCHES * QC, C)
+    def cost_chunk(q):
+        block = ordered[:, q * (QC // 8):(q + 1) * (QC // 8)].reshape(PATCHES * QC, C)
         a, b = halves(block)
         part = nt16(jnp.concatenate([a, a, b], axis=1), scat[...])
         cost[q] = part.reshape(PATCHES, QC, BAND)
-        return 0
 
     def join(values):
         top = functools.reduce(jnp.maximum, [a for a, _ in values])
         scales = [jnp.exp(a - top) for a, _ in values]
         return top, sum(b * f for (_, b), f in zip(values, scales)), scales
 
-    lax.fori_loop(0, PARTS, cost_chunk, 0)
+    cost_chunk(0)
     m1.wait_recv()
     top, tot, scales = join([(st[0], st[1]), (st_core[0], st_core[1])])
     fac[0] = scales[0]
@@ -214,7 +210,7 @@
                 return tuple(new)
 
             zero = tuple(jnp.zeros((8, 128), F32) for _ in range(QC // 8 * K))
-            acc = lax.fori_loop(0, PATCHES, step, zero, unroll=8)
+            acc = lax.fori_loop(0, PATCHES, step, zero, unroll=True)
             for k in range(K):
                 for g in range(QC // 8):
                     zc[i, k, g * 8:g * 8 + 8, cols] = acc[k * (QC // 8) + g]
@@ -235,13 +231,27 @@
         st_h[0, 1:2, :] = tot
         return [send(st_h.at[0], st_h.at[1 + i], who) for i, who in enumerate(h_peer)], scales
 
+    cost_chunk(1)
     core = [sums(0)]
     over = []
     for i in range(1, PARTS):
+        if i + 1 < PARTS:
+            cost_chunk(i + 1)
         core.append(sums(i))
         over.append(over_x(i - 1, core[i - 1]))
     over.append(over_x(PARTS - 1, core[PARTS - 1]))
     m3, x_scales = x_stats()
+
+    def over_h(i, came):
+        for one in came:
+            one.wait_recv()
+        total = zx[i, x] * x_scales[0]
+        for j in range(NX - 1):
+            total = total + x_in[i, j] * x_scales[1 + j]
+        zh[i] = total
+        return [send(zh.at[i], h_in.at[i, j], who) for j, who in enumerate(h_peer)]
+
+    d = [over_h(i, came) for i, came in enumerate(over)]
     pv = nn(pw[...], vm[...])
     bv = nn(pb[...], vm[...])
     pk = nn(pv, wk[...])
@@ -267,17 +277,12 @@
     q_ids = jnp.sum(jnp.where(picked, id_rows[1], 0.0), axis=1, keepdims=True)
     choose = jnp.where(picked, 1.0, 0.0).astype(F32)
 
-
-    def over_h(i, came):
-        for one in came:
-            one.wait_recv()
-        total = zx[i, x] * x_scales[0]
-        for j in range(NX - 1):
-            total = total + x_in[i, j] * x_scales[1 + j]
-        zh[i] = total
-        return [send(zh.at[i], h_in.at[i, j], who) for j, who in enumerate(h_peer)]
-
-    d = [over_h(i, came) for i, came in enumerate(over)]
+    for ref, cat in ((up, up_cat), (down, down_cat)):
+        n = ref.shape[0]
+        a, b = halves(ref[...])
+        cat[0:n, :] = a
+        cat[n:2 * n, :] = b
+        cat[2 * n:3 * n, :] = a
     for one in m3:
         one.wait_recv()
     _, tot, h_scales = join([(st_h[i, 0:1, :], st_h[i, 1:2, :]) for i in range(NH)])
@@ -301,9 +306,10 @@
     qa = nn(zq, wq_all) + cq_all
     qz = qa[:, 0:PATCH]
     qb = qa[:, PATCH:PATCH + 1]
+    middle = nn(qz, zt[1])
     for one in f:
         one.wait_recv()
-    logits = jnp.concatenate([nn(qz, zt[b]) for b in range(3)], axis=1) + qb
+    logits = jnp.concatenate([nn(qz, zt[0]), middle, nn(qz, zt[2])], axis=1) + qb
     same = q_ids == jnp.concatenate(id_rows, axis=1)
     logits = jnp.where(same, logits, -jnp.inf)
     attend = jnp.exp(logits - jnp.max(logits, axis=1, keepdims=True))
@@ -313,22 +319,22 @@
     center = jnp.mean(resid, axis=-1, keepdims=True)
     var = jnp.mean((resid - center) ** 2, axis=-1, keepdims=True)
     normed = (resid - center) / jnp.sqrt(var + 1e-05) * gain[...]
-    hidden = jax.nn.gelu(nn(normed, up[...]) + upb[...])
-    fin_out[...] = resid + nn(hidden, down[...])
-
+    hidden = jax.nn.gelu(nn3(normed, up_cat[...]) + upb[...])
+    fin_out[...] = resid + nn3(hidden, down_cat[...])
+
+    early = len(sends)
     g = []
-    for d in range(1, NX):
-        rows = pl.ds(pl.multiple_of((c * NX + xs[d - 1]) * ROWS, ROWS), ROWS)
-        g.append(send(fin_out.at[rows], fin_in.at[mine], x_peer[d - 1]))
-    for d in range(NX):
-        rows = pl.ds(pl.multiple_of(((1 - c) * NX + (x + d) % NX) * ROWS, ROWS), ROWS)
-        g.append(send(fin_out.at[rows], fin_in.at[mine], sib if d == 0 else o_peer[d - 1]))
+    for i, cc in ((1, 1 - c), (2, 1 - c), (3, 1 - c), (1, c), (2, c), (3, c), (0, 1 - c)):
+        rows = pl.ds(pl.multiple_of((cc * NX + (x + i) % NX) * ROWS, ROWS), ROWS)
+        g.append(send(fin_out.at[rows], fin_in.at[mine], (band, tid((x + i) % NX, h, cc))))
+    for one in sends[:early]:
+        one.wait_send()
     fin_in[mine] = fin_out[pl.ds(pl.multiple_of(mine * ROWS, ROWS), ROWS)]
     for one in g:
         one.wait_recv()
     for k in range(K):
         out[:, k, :] = fin_in[k]
-    for one in sends:
+    for one in g:
         one.wait_send()
 
 
@@ -342,7 +348,7 @@
     bands = lax.axis_size("src")
     tiles = target_feat.reshape(TARGETS // 8, 8, 2, 128).transpose(0, 2, 1, 3).reshape(2 * TARGETS, 128)
     params = (
-        source_feat, target_order.reshape(32, 128), window_id.reshape(16, 128),
+        target_order.reshape(32, 128), window_id.reshape(16, 128),
         latent_query, patch_weight, patch_embed_bias.reshape(1, -1), key_weight, value_matrix, window_query, window_key,
         window_value, window_out, norm_gain.reshape(1, -1), up_weight, up_bias.reshape(1, -1), down_weight,
     )
@@ -371,9 +377,12 @@
         pltpu.VMEM((PARTS, QC, BAND), F32),
         pltpu.VMEM((PARTS, NH - 1, QC, BAND), F32),
         pltpu.VMEM((3, PATCH, BAND), F32),
+        pltpu.VMEM((3 * D, 512), jnp.bfloat16),
+        pltpu.VMEM((3 * 512, D), jnp.bfloat16),
         pltpu.VMEM((PIX, D), F32),
         pltpu.VMEM((K, ROWS, D), F32),
         pltpu.SemaphoreType.DMA((len(params),)),
+        pltpu.SemaphoreType.DMA,
         pltpu.SemaphoreType.DMA,
         pltpu.SemaphoreType.DMA,
         pltpu.SemaphoreType.DMA((COPIES,)),
@@ -382,14 +391,14 @@
     return pl.pallas_call(
         functools.partial(kernel, bands),
         out_shape=jax.ShapeDtypeStruct((ROWS, K, D), F32),
-        in_specs=[hbm] * (1 + len(params)),
+        in_specs=[hbm] * (2 + len(params)),
         out_specs=vmem,
         scratch_shapes=scratch,
         compiler_params=pltpu.CompilerParams(
             collective_id=0, has_side_effects=True, vmem_limit_bytes=60 * 1024 * 1024
         ),
         name="encode",
-    )(tiles, *params)
+    )(tiles, source_feat, *params)
 
 
 def solution(mesh):

time: 52 us -> 49.6 us (0.954)
  Pallas kernels: 50.5 us -> 48 us
    pallas_call x1, Pallas kernels: 50.5 us -> 48 us  [local(): pl.pallas_call(functools.partial(kernel, bands), out_shape=jax.ShapeDtype...]
where the time goes in v3:
time: 49.6 us; the launch traced here: 49.4 us
  Pallas kernels  48 us (97%)
  local copies, waits for them, and re-layouts  1.38 us (3%)
    pallas_call x1, Pallas kernels, local(): pl.pallas_call(functools.partial(kernel, bands), out_shape=jax.ShapeDtype...  48 us
    unnamed x1, local copies, waits for them, and re-layouts  1.38 us

profile of v3, /device:TPU:1, one launch (start us, length us, event | category | flops | bytes accessed | tf_op | source)
XLA Modules:
  0.0 49.4 jit_solution(12797029358089175974)
XLA Ops:
  0.0 48.0 %encode.1 = f32[8,8,128]{2,1,0:T(8,128)} custom-call(f32[8192,128]{1,0:T(8,128)} %bitcast.10, f32[8,256]{1,0:T(8,128)} %src_h.1, s32[32,128]{1,0:T(8,128)} %bitcast.11, s32[16,128]{1,0:T(8,128)} %bitcast.12, f32[8,128]{1,0:T(8,128)} %lq_h.1, f32[64,128]{1,0:T(8,128)} %pw_h.1, f32[1,128]{1,0:T(1,128)} %bitcast.14, f32[128,128]{1,0:T(8,128)} %kw_h.1, ...), custom_call_target="tpu_custom_call" | custom-call | tf_op jit(solution)/shard_map/encode/pallas_call | solution.py:391
  48.0 1.4 %copy.19 = f32[8,8,128]{2,1,0:T(8,128)} copy(f32[8,8,128]{2,1,0:T(8,128)} %encode.1) | data formatting | bytes 65536

commit v4 on v3

--- a/solution.py
+++ b/solution.py
@@ -69,8 +69,8 @@
         return (xx * NH + hh) * NC + cc
 
     sib = (band, tid(x, h, 1 - c))
-    xs = [(x + d) % NX for d in range(1, NX)]
-    hs = [(h + d) % NH for d in range(1, NH)]
+    xs = [(x + d) % NX for d in (2, 1, 3)]
+    hs = [(h + d) % NH for d in (2, 1, 3)]
     x_peer = [(band, tid(xx, h, c)) for xx in xs]
     h_peer = [(band, tid(x, hh, c)) for hh in hs]
     o_peer = [(band, tid((x + d) % NX, h, 1 - c)) for d in range(1, NX)]

time: 49.6 us -> 49.8 us (level)
  no operation moved by 1% of the time
where the time goes in v4:
time: 49.8 us; the launch traced here: 49.7 us
  Pallas kernels  48.3 us (97%)
  local copies, waits for them, and re-layouts  1.38 us (3%)
    pallas_call x1, Pallas kernels, local(): pl.pallas_call(functools.partial(kernel, bands), out_shape=jax.ShapeDtype...  48.3 us
    unnamed x1, local copies, waits for them, and re-layouts  1.38 us

profile of v4, /device:TPU:1, one launch (start us, length us, event | category | flops | bytes accessed | tf_op | source)
XLA Modules:
  0.0 49.7 jit_solution(5048139896015351890)
XLA Ops:
  0.0 48.3 %encode.1 = f32[8,8,128]{2,1,0:T(8,128)} custom-call(f32[8192,128]{1,0:T(8,128)} %bitcast.10, f32[8,256]{1,0:T(8,128)} %src_h.1, s32[32,128]{1,0:T(8,128)} %bitcast.11, s32[16,128]{1,0:T(8,128)} %bitcast.12, f32[8,128]{1,0:T(8,128)} %lq_h.1, f32[64,128]{1,0:T(8,128)} %pw_h.1, f32[1,128]{1,0:T(1,128)} %bitcast.14, f32[128,128]{1,0:T(8,128)} %kw_h.1, ...), custom_call_target="tpu_custom_call" | custom-call | tf_op jit(solution)/shard_map/encode/pallas_call | solution.py:391
  48.3 1.4 %copy.19 = f32[8,8,128]{2,1,0:T(8,128)} copy(f32[8,8,128]{2,1,0:T(8,128)} %encode.1) | data formatting | bytes 65536
